TPU v7x, 32 devices: a whole 2x2x4 slice. The times are simulated.
32 devices in a mesh: ctx: 4 (over z), ch: 8 (over y, x, core).
Axes of the slice: x: 2, y: 2, z: 4, core: 2. Of those that a mesh axis runs over, the one named last changes fastest.
Arguments:
- features: bfloat16 [3, 1024, 8192], P(None, 'ctx', 'ch'), may hold values from -6 to 6
- short_weight: float32 [3, 7, 8192], P(None, None, 'ch'), may hold values from -2 to 2
- rates: float32 [8192, 16], P('ch'), may hold values from 0.00029296876 to 0.08
- residues: float32 [8192, 16], P('ch'), may hold values from -0.75 to 0.75
- skip: float32 [8192], P('ch'), may hold values from -4 to 4
- out_weight: bfloat16 [8192, 8192], P('ctx', 'ch'), may hold values from -0.0625 to 0.0625
Outputs:
- mixed: bfloat16 [1024, 8192], P('ctx', 'ch')
All inputs are finite; a program needn't handle non-finite values.
Results may differ from a plain program's by a relative error of at most 0.0076.
Values may be sent and summed in bfloat16 or wider, within the bound.
A program may use at most 128 MiB of HBM per device.

v0:
```python
import jax
import jax.numpy as jnp
from jax import lax
from jax.sharding import PartitionSpec as P

STRETCH = 64


def passed_along(value, axis, by):
    length = lax.axis_size(axis)
    pairs = [(i, i + by) for i in range(length) if 0 <= i + by < length]
    return lax.ppermute(value, axis, pairs)


def prefix_2(value, axis, combine, identity):
    length, place = (lax.axis_size(axis), lax.axis_index(axis))
    everything = jax.tree.map(lambda part: lax.all_gather(part, axis), value)
    start = jax.tree.map(
        lambda part, zero: jnp.broadcast_to(jnp.asarray(zero, part.dtype), part.shape),
        value,
        identity,
    )

    def lap(k, before):
        reached = k < place
        new = combine(before, jax.tree.map(lambda part: part[k], everything))
        return jax.tree.map(lambda a, b: jnp.where(reached, a, b), new, before)

    return lax.fori_loop(0, length, lap, start)


def join_states(earlier, later):
    return (earlier[0] * later[0], earlier[1] * later[0] + later[1])


def per_device(features, short_weight, rates, residues, skip, out_weight):
    kernel_width = short_weight.shape[1]
    local_rows = features.shape[1]
    local_chans = features.shape[2]
    highest = lax.Precision.HIGHEST
    left_rim = passed_along(features[:, local_rows - (kernel_width - 1) :, :], "ctx", 1)
    extended = jnp.concatenate([left_rim, features], axis=1).astype(jnp.float32)
    featured = jnp.zeros((3, local_rows, local_chans), jnp.float32)
    for offset in range(kernel_width):
        featured = (
            featured
            + short_weight[:, offset][:, None, :]
            * extended[:, kernel_width - 1 - offset : kernel_width - 1 - offset + local_rows, :]
        )
    featured = featured.astype(jnp.bfloat16)
    query = featured[0].astype(jnp.float32)
    product = (featured[1].astype(jnp.float32) * featured[2].astype(jnp.float32)).astype(
        jnp.bfloat16
    )
    product_value = product.astype(jnp.float32)
    block_count = local_rows // STRETCH
    decay_rate = rates.T
    mode_gain = residues.T
    block_lag = jnp.arange(STRETCH, dtype=jnp.float32)
    block_index = jnp.arange(STRETCH, dtype=jnp.int32)
    short_filter = jnp.einsum(
        "nc,nca->ca",
        mode_gain,
        jnp.exp(-decay_rate[:, :, None] * block_lag[None, None, :]),
        precision=highest,
    )
    lag_table = block_index[:, None] - block_index[None, :]
    toeplitz = jnp.where(
        (lag_table >= 0)[None, :, :], short_filter[:, jnp.maximum(lag_table, 0)], 0.0
    )
    blocks = product_value.reshape(block_count, STRETCH, local_chans)
    inner_part = jnp.einsum("cab,kbc->kac", toeplitz, blocks, precision=highest)
    to_block_end = jnp.exp(-decay_rate[None, :, :] * (STRETCH - 1 - block_lag)[:, None, None])
    block_states = jnp.einsum("kbc,bnc->knc", blocks, to_block_end, precision=highest)
    block_decay = jnp.exp(-decay_rate * STRETCH)

    def advance(state_now, block_state):
        return (block_decay * state_now + block_state, state_now)

    local_total, states_before = lax.scan(advance, jnp.zeros_like(decay_rate), block_states)
    span_decay = jnp.exp(-decay_rate * local_rows)
    prefix = prefix_2(
        (span_decay, local_total),
        "ctx",
        join_states,
        (jnp.ones_like(decay_rate), jnp.zeros_like(decay_rate)),
    )
    incoming = prefix[1]
    block_offset = jnp.arange(block_count, dtype=jnp.float32) * STRETCH
    start_states = (
        jnp.exp(-decay_rate[None, :, :] * block_offset[:, None, None]) * incoming[None, :, :]
        + states_before
    )
    mode_output = mode_gain[None, :, :] * jnp.exp(
        -decay_rate[None, :, :] * (block_lag + 1.0)[:, None, None]
    )
    outer_part = jnp.einsum("knc,anc->kac", start_states, mode_output, precision=highest)
    conv_value = (inner_part + outer_part).reshape(local_rows, local_chans) + skip[
        None, :
    ] * product_value
    gated = (query * conv_value).astype(jnp.bfloat16)
    whole_rows = lax.all_gather(gated, "ch", axis=1, tiled=True)
    mixed = jnp.dot(
        whole_rows,
        lax.all_gather(out_weight, "ctx", axis=0, tiled=True),
        preferred_element_type=jnp.float32,
    )
    return mixed.astype(jnp.bfloat16)


def solution(mesh):
    return jax.shard_map(
        per_device,
        mesh=mesh,
        in_specs=(
            P(None, "ctx", "ch"),
            P(None, None, "ch"),
            P("ch", None),
            P("ch", None),
            P("ch"),
            P("ctx", "ch"),
        ),
        out_specs=P("ctx", "ch"),
        check_vma=False,
    )
```

profile of v0, /device:TPU:8, one launch (start us, length us, event | category | flops | bytes accessed | tf_op | source)
XLA Modules:
  0.0 503.3 jit_solution(8891685839900986120)
XLA Ops:
  6.5 0.0 all-gather.5.cloned.1.call-start
  6.5 0.8 slice.55
  7.4 3.5 collective-permute-start
  10.9 0.8 negate_bitcast_fusion
  11.7 0.9 multiply_exponential_fusion.1
  12.6 1.5 fusion.34
  14.1 0.1 reshape.74
  14.3 1.6 multiply_reduce_fusion
  15.8 12.8 %all-gather = f32[64,1024]{1,0:T(8,128)} all-gather(f32[16,1024]{1,0:T(8,128)S(1)} %get-tuple-element.208), channel_id=2, replica_groups=mesh['ctx'=4,'ch'=8] {'ctx'}, dimensions={0}, use_global_device_ids=true | all-gather | bytes 327680 | tf_op jit(solution)/shard_map/all_gather | solution.py:17
  28.7 1.0 copy.26
  29.7 18.5 %gather_fusion = f32[4096,1024]{1,0:T(8,128)} fusion(f32[1024,64]{0,1:T(8,128)S(1)} %multiply_reduce_fusion, s32[4096]{0:T(1024)S(1)} %broadcast_clamp_fusion), kind=kCustom, calls=%fused_computation | custom fusion | bytes 33570816 | tf_op jit(solution)/shard_map/gather | solution.py:69
  48.2 0.0 copy-start.5
  48.2 30.6 %copy.23 = f32[64,64,1024]{1,0,2:T(8,128)} copy(f32[64,64,1024]{2,1,0:T(8,128)} %bitcast.76) | data formatting | bytes 33554432 | tf_op jit(solution)/shard_map/gather | solution.py:69
  78.8 0.0 copy-done.5
  78.8 1.0 copy.25
  79.8 0.0 collective-permute-done
  79.8 0.0 copy-done.1
  79.8 0.5 maximum_convert_fusion
  80.3 2.7 fusion.19
  83.0 0.2 multiply_convert_fusion
  83.2 0.7 copy.24
  83.9 0.0 copy-start.4
  83.9 10.2 %fusion.27 = f32[4,16,1024]{1,0,2:T(4,128)} fusion(bf16[4,64,1024]{1,0,2:T(4,128)(2,1)S(1)} %copy.24, f32[64]{0:T(128)S(1)} %iota_subtract_fusion, f32[16,1024]{0,1:T(8,128)} %copy.26), kind=kOutput, calls=%fused_computation.39 | convolution fusion | flops 51380224 | bytes 852224 | tf_op jit(solution)/shard_map/kbc,bnc->knc/dot_general | solution.py:74
  94.1 1.8 copy.28
  96.0 0.0 copy-done.4
  96.0 0.3 while.27
  96.2 14.1 %all-gather.1 = f32[64,1024]{1,0:T(8,128)S(1)} all-gather(f32[16,1024]{1,0:T(8,128)S(1)} %get-tuple-element.127), channel_id=3, replica_groups=mesh['ctx'=4,'ch'=8] {'ctx'}, dimensions={0}, use_global_device_ids=true | all-gather | bytes 327680 | tf_op jit(solution)/shard_map/all_gather | solution.py:17
  110.3 3.6 while.28
  110.3 0.9 fusion.41
  111.2 0.9 fusion.41
  112.1 0.9 fusion.41
  113.0 0.9 fusion.41
  113.9 0.1 multiply_add_fusion
  114.0 1.7 copy.29
  115.7 30.0 %fusion.1 = f32[1024,4,64]{2,1,0:T(4,128)S(1)} fusion(bf16[4,64,1024]{1,0,2:T(4,128)(2,1)S(1)} %copy.24, f32[64,64,1024]{1,0,2:T(8,128)} %copy.23, pred[64,64]{1,0:T(8,128)(4,1)S(1)} %subtract_compare_fusion), kind=kOutput, calls=%fused_computation.6 | convolution fusion | flops 205520896 | bytes 18354176 | tf_op jit(solution)/shard_map/cab,kbc->kac/dot_general | solution.py:72
  145.7 0.0 copy-done
  145.7 0.0 copy-done.2
  145.7 0.0 copy-done.3
  145.7 12.1 %bitcast_add_fusion.2 = f32[4,64,1024]{1,0,2:T(4,128)} fusion(f32[1024,4,64]{2,1,0:T(4,128)S(1)} %fusion.1, f32[4,16,1024]{1,0,2:T(4,128)S(1)} %copy-done, f32[64]{0:T(128)S(1)} %iota_add_fusion, f32[16,1024]{0,1:T(8,128)S(1)} %copy-done.2, f32[16,1024]{0,1:T(8,128)S(1)} %copy-done.3), kind=kOutput, calls=%fused_computation.38 | convolution fusion | flops 52690944 | bytes 2490624 | tf_op jit(solution)/shard_map/knc,anc->kac/dot_general | solution.py:97
  157.8 1.9 copy.30
  159.7 0.0 copy-done.6
  159.7 1.1 fusion.32
  160.8 0.0 all-gather.5.cloned.1.call-update
  160.9 0.3 all-gather.7.cloned.1.call-start
  161.1 0.5 all-gather.7.cloned.1.call-update
  161.6 37.1 %all-gather.5.cloned.1.call-done = bf16[256,8192]{1,0:T(8,128)(2,1)} async-done(((bf16[256,1024]{1,0:T(8,128)(2,1)}), bf16[256,8192]{1,0:T(8,128)(2,1)}) %all-gather.5.cloned.1.call-update) | async-done | bytes 4194320 | tf_op jit(solution)/shard_map/all_gather | solution.py:102
  198.8 285.4 %all-gather.7.cloned.1.call-done = bf16[8192,1024]{1,0:T(8,128)(2,1)} async-done(((bf16[2048,1024]{1,0:T(8,128)(2,1)}), bf16[8192,1024]{1,0:T(8,128)(2,1)}) %all-gather.7.cloned.1.call-update) | async-done | bytes 16777232 | tf_op jit(solution)/shard_map/all_gather | solution.py:105
  484.1 12.3 %convolution_convert_fusion = bf16[256,1024]{1,0:T(8,128)(2,1)} fusion(bf16[256,8192]{1,0:T(8,128)(2,1)} %all-gather.5.cloned.1.call-done, bf16[8192,1024]{1,0:T(8,128)(2,1)} %all-gather.7.cloned.1.call-done), kind=kOutput, calls=%fused_computation.41 | convolution fusion | flops 4295229440 | bytes 21495808 | tf_op jit(solution)/shard_map/dot_general | solution.py:103
  (26 shorter events, 0.2 us)
Async XLA Ops:
  6.5 192.2 %all-gather.5.cloned.1.call-start = ((), (), s32[]{:S(2)}) async-start(), calls=%async_computation | async-start | bytes 4718592 | tf_op jit(solution)/shard_map/all_gather | solution.py:102
  7.4 72.5 %collective-permute-start = (bf16[3,6,1024]{2,1,0:T(8,128)(2,1)S(1)}, bf16[3,6,1024]{2,1,0:T(8,128)(2,1)S(1)}, u32[]{:S(2)}, u32[]{:S(2)}) collective-permute-start(bf16[3,6,1024]{2,1,0:T(8,128)(2,1)S(1)} %slice.55), channel_id=1, source_target_pairs={{0,8},{8,16},{16,24},{1,9},{9,17},{17,25},{2,10},{10,18},{18,26},{... | collective-permute-start | bytes 110600 | tf_op jit(solution)/shard_map/ppermute | solution.py:12
  48.2 30.6 %copy-start.5 = (f32[1024,16]{0,1:T(8,128)S(1)}, f32[1024,16]{0,1:T(8,128)}, u32[]{:S(2)}) copy-start(f32[1024,16]{0,1:T(8,128)} %param.13) | copy-start | bytes 196612
  48.2 31.6 %copy-start.1 = (bf16[3,256,1024]{2,1,0:T(8,128)(2,1)S(1)}, bf16[3,256,1024]{2,1,0:T(8,128)(2,1)}, u32[]{:S(2)}) copy-start(bf16[3,256,1024]{2,1,0:T(8,128)(2,1)} %param.10) | copy-start | bytes 4718596
  83.9 12.1 %copy-start.4 = (f32[4,16,1024]{2,1,0:T(8,128)S(1)}, f32[4,16,1024]{2,1,0:T(8,128)}, u32[]{:S(2)}) copy-start(f32[4,16,1024]{2,1,0:T(8,128)} %custom-call.4) | copy-start | bytes 786436
  115.7 30.0 %copy-start = (f32[4,16,1024]{1,0,2:T(4,128)S(1)}, f32[4,16,1024]{1,0,2:T(4,128)}, u32[]{:S(2)}) copy-start(f32[4,16,1024]{1,0,2:T(4,128)} %copy.29) | copy-start | bytes 786436
  115.7 30.0 %copy-start.2 = (f32[16,1024]{0,1:T(8,128)S(1)}, f32[16,1024]{0,1:T(8,128)}, u32[]{:S(2)}) copy-start(f32[16,1024]{0,1:T(8,128)} %copy.26) | copy-start | bytes 196612
  115.7 30.0 %copy-start.3 = (f32[16,1024]{0,1:T(8,128)S(1)}, f32[16,1024]{0,1:T(8,128)}, u32[]{:S(2)}) copy-start(f32[16,1024]{0,1:T(8,128)} %copy.25) | copy-start | bytes 196612
  157.8 1.9 copy-start.6
  160.9 323.3 %all-gather.7.cloned.1.call-start = ((), (), s32[]{:S(2)}) async-start(), calls=%async_computation.1 | async-start | bytes 20971520 | tf_op jit(solution)/shard_map/all_gather | solution.py:105
Sparse Core Ops, SparseCore 0:
  161.0 37.7 all-gather.4
  200.3 283.7 all-gather.6
where the time goes:
time: 509 us; the launch traced here: 503 us
  waiting for transfers between devices  323 us (63%)
  matrix products  64.6 us (13%)
  local copies, waits for them, and re-layouts  59.7 us (12%)
  blocking collectives  26.9 us (5%)
  between operations  13.6 us (3%)
  other arithmetic  11.5 us (2%)
    all_gather x1, waiting for transfers between devices, per_device(): lax.all_gather(out_weight, 'ctx', axis=0, tiled=True)  285 us
    gather x2, local copies, waits for them, and re-layouts, per_device(): short_filter[:, jnp.maximum(lag_table, 0)]  49.1 us
    all_gather x1, waiting for transfers between devices, per_device(): whole_rows = lax.all_gather(gated, 'ch', axis=1, tiled=True)  37.1 us
    dot_general x1, matrix products, per_device(): inner_part = jnp.einsum('cab,kbc->kac', toeplitz, blocks, precision=highest)  30 us
    all_gather x2, blocking collectives, prefix_2(): everything = jax.tree.map(lambda part: lax.all_gather(part, axis), value)  26.9 us
    dot_general x1, matrix products, per_device(): jnp.dot(whole_rows, lax.all_gather(out_weight, 'ctx', axis=0, tiled=True)...  12.3 us
    dot_general x1, matrix products, per_device(): jnp.einsum('knc,anc->kac', start_states, mode_output, precision=highest)  12.1 us
    dot_general x1, matrix products, per_device(): jnp.einsum('kbc,bnc->knc', blocks, to_block_end, precision=highest)  10.2 us
  transfers between devices with their start and end apart: 3, of which 2 were waited for; matrix products, arithmetic and copies ran while one was open for 11% of the time, Pallas kernels for 0%

commit v1 on v0

v1 whole, which is shorter than its diff:
```python
import functools
import jax
import jax.numpy as jnp
from jax import lax
from jax.experimental import pallas as pl
from jax.experimental.pallas import tpu as pltpu
from jax.sharding import PartitionSpec as P

MESH = pl.DeviceIdType.MESH
LANES = 128
HEAD = 8
RIM = 16
UNROLL = 8


def each(low, high, body):
    if high - low <= 8:
        for i in range(low, high):
            body(i)
    else:

        def step(i, carry):
            body(i)
            return carry

        lax.fori_loop(low, high, step, 0)


def remote(src, dst, send_sem, recv_sem, device):
    return pltpu.make_async_remote_copy(
        src_ref=src,
        dst_ref=dst,
        send_sem=send_sem,
        recv_sem=recv_sem,
        device_id=device,
        device_id_type=MESH,
    )


def rounded(value):
    return value.astype(jnp.bfloat16).astype(jnp.float32)


def added(terms):
    while len(terms) > 1:
        terms = [a + b for a, b in zip(terms[::2], terms[1::2])] + (
            [terms[-1]] if len(terms) % 2 else []
        )
    return terms[0]


def operator_kernel(
    nz, modes, width,
    feat_ref, taps_ref, rates_ref, gains_ref, skip_ref,
    out_ref,
    rim, wide, product, query, gated, total, states,
    rim_send, rim_recv, state_send, state_recv,
):
    z, c = lax.axis_index("ctx"), lax.axis_index("ch")
    tokens, chans = feat_ref.shape[1], feat_ref.shape[2]
    subs = chans // LANES
    parts, rows = out_ref.shape[0], out_ref.shape[1]

    barrier = pltpu.get_barrier_semaphore()

    def greet(d):
        pl.semaphore_signal(
            barrier, inc=1, device_id=(lax.rem(z + d, nz), c), device_id_type=MESH
        )

    each(1, nz, greet)
    pl.semaphore_wait(barrier, nz - 1)

    rim_copy = remote(
        feat_ref.at[:, pl.ds(tokens - RIM, RIM), :], rim, rim_send, rim_recv,
        (lax.rem(z + 1, nz), c),
    )

    @pl.when(z < nz - 1)
    def _():
        rim_copy.start()

    for s in range(3):
        for g in range(subs):
            wide[s, pl.ds(HEAD * subs + g, tokens, stride=subs), :] = feat_ref[
                s, :, g * LANES : (g + 1) * LANES
            ].astype(jnp.float32)

    @pl.when(z > 0)
    def _():
        rim_copy.wait_recv()
        for s in range(3):
            for g in range(subs):
                part = rim[s, :, g * LANES : (g + 1) * LANES].astype(jnp.float32)
                wide[s, pl.ds(g, HEAD, stride=subs), :] = part[RIM - HEAD :, :]

    @pl.when(z == 0)
    def _():
        wide[:, pl.ds(0, HEAD * subs), :] = jnp.zeros((3, HEAD * subs, LANES), jnp.float32)

    def at(n):
        return pl.ds(n * subs, subs)

    def token(t):
        return pl.ds(pl.multiple_of(t * subs, subs), subs)

    def featured(s, t, weights):
        value = weights[0] * wide[s, token(t + HEAD), :]
        for j in range(1, width):
            value = value + weights[j] * wide[s, token(t + HEAD - j), :]
        return rounded(value)

    def taps_of(s):
        return [taps_ref[at(s * width + j), :] for j in range(width)]

    decay = [jnp.exp(-rates_ref[at(n), :]) for n in range(modes)]
    taps_1, taps_2 = taps_of(1), taps_of(2)

    def first(i, carry):
        carry = list(carry)
        for u in range(UNROLL):
            t = i * UNROLL + u
            value = rounded(featured(1, t, taps_1) * featured(2, t, taps_2))
            product[token(t), :] = value
            carry = [k * m + value for k, m in zip(decay, carry)]
        return tuple(carry)

    zero = jnp.zeros((subs, LANES), jnp.float32)
    ends = lax.fori_loop(0, tokens // UNROLL, first, (zero,) * modes)
    for n in range(modes):
        total[at(n), :] = ends[n]

    def pass_on(d):
        @pl.when(z + d < nz)
        def _():
            remote(
                total, states.at[d - 1], state_send.at[d - 1], state_recv.at[d - 1],
                (lax.rem(z + d, nz), c),
            ).start()

    each(1, nz, pass_on)

    taps_0 = taps_of(0)

    def second(i, carry):
        for u in range(UNROLL):
            t = i * UNROLL + u
            query[token(t), :] = featured(0, t, taps_0)
        return carry

    lax.fori_loop(0, tokens // UNROLL, second, 0)

    def arrive(d):
        @pl.when(z >= d)
        def _():
            remote(
                total, states.at[d - 1], state_send.at[d - 1], state_recv.at[d - 1],
                (lax.rem(z + d, nz), c),
            ).wait_recv()

        @pl.when(z < d)
        def _():
            states[d - 1] = jnp.zeros((modes * subs, LANES), jnp.float32)

    each(1, nz, arrive)

    incoming = []
    for n in range(modes):
        span = jnp.exp(-rates_ref[at(n), :] * float(tokens))
        value = states[nz - 2, at(n), :]
        for d in range(nz - 2, 0, -1):
            value = value * span + states[d - 1, at(n), :]
        incoming.append(value)

    gains = [gains_ref[at(n), :] for n in range(modes)]
    skip = skip_ref[...]

    def third(i, carry):
        carry = list(carry)
        for u in range(UNROLL):
            t = i * UNROLL + u
            value = product[token(t), :]
            carry = [k * m + value for k, m in zip(decay, carry)]
            conv = added([g * m for g, m in zip(gains, carry)] + [skip * value])
            gated[token(t), :] = query[token(t), :] * conv
        return tuple(carry)

    lax.fori_loop(0, tokens // UNROLL, third, tuple(incoming))

    for j in range(parts):
        for g in range(subs):
            out_ref[j, :, g * LANES : (g + 1) * LANES] = gated[
                pl.ds(j * rows * subs + g, rows, stride=subs), :
            ].astype(jnp.bfloat16)

    @pl.when(z < nz - 1)
    def _():
        rim_copy.wait_send()

    def leave(d):
        @pl.when(z + d < nz)
        def _():
            remote(
                total, states.at[d - 1], state_send.at[d - 1], state_recv.at[d - 1],
                (lax.rem(z + d, nz), c),
            ).wait_send()

    each(1, nz, leave)


def project_kernel(
    nz, nc,
    g_ref, w_ref,
    out_ref,
    weights, stage, blocks, sent, taken, own,
    w_sem, a_send, a_recv, b_send, b_recv, s_send, s_recv, m_send, m_recv, p_send, p_recv,
):
    z, c = lax.axis_index("ctx"), lax.axis_index("ch")
    fold = nc // nz
    chips = nc // 2
    chip, core = c // 2, lax.rem(c, 2)
    mate = c + 1 - 2 * core
    tokens, columns = out_ref.shape
    rows, chans = g_ref.shape[1], g_ref.shape[2]
    tile = min(columns, 256)

    barrier = pltpu.get_barrier_semaphore()

    def greet_plane(i):
        pl.semaphore_signal(
            barrier, inc=1, device_id=(z, lax.rem(c + i, nc)), device_id_type=MESH
        )

    def greet_line(d):
        pl.semaphore_signal(
            barrier, inc=1, device_id=(lax.rem(z + d, nz), c), device_id_type=MESH
        )

    each(1, nc, greet_plane)
    each(1, nz, greet_line)
    pl.semaphore_wait(barrier, nc + nz - 2)

    w_copy = pltpu.make_async_copy(w_ref, weights, w_sem)

    def scatter(i):
        j = lax.rem(c + i, nc)
        return remote(g_ref.at[j], stage.at[c], a_send.at[i], a_recv.at[c], (z, j))

    each(1, nc, lambda i: scatter(i).start())
    own_part = pltpu.make_async_copy(g_ref.at[c], stage.at[c], a_recv.at[c])
    own_part.start()
    w_copy.start()

    def plane(d):
        return lax.rem(z + d, nz)

    def along(d):
        q = plane(d)
        src = stage.at[pl.ds(q * fold, fold)]
        dst = blocks.at[z, :, c]
        if d == nz:
            return pltpu.make_async_copy(src, dst, b_recv.at[z])
        return remote(src, dst, b_send.at[d], b_recv.at[z], (q, c))

    for d in range(1, nz + 1):
        for m in range(fold):
            k = plane(d) * fold + m
            pltpu.make_async_copy(g_ref.at[0], stage.at[k], a_recv.at[k]).wait()
        along(d).start()

    def piece(k, j):
        return blocks.at[k, :, j]

    def spread(d, i):
        k = plane(d)
        to = lax.rem(chip + i, chips) * 2 + core
        return remote(piece(k, c), piece(k, c), s_send.at[d - 1, i], s_recv.at[k, chip], (z, to))

    def hand(d, i):
        k = plane(d)
        p = lax.rem(chip + i, chips)
        j = p * 2 + core
        return remote(piece(k, j), piece(k, j), m_send.at[d - 1, i], m_recv.at[k, p], (z, mate))

    def back(d):
        return remote(
            sent.at[d - 1], taken.at[d - 1], p_send.at[d - 1], p_recv.at[d - 1], (plane(d), c)
        )

    def multiply(d):
        k = plane(d)

        def strip(i):
            cols = pl.ds(pl.multiple_of(i * tile, tile), tile)
            value = jnp.zeros((tokens, tile), jnp.float32)
            for m in range(fold):
                left = blocks[k, m]
                if rows % 16:
                    left = left.astype(jnp.float32).reshape(tokens, chans).astype(jnp.bfloat16)
                else:
                    left = left.reshape(tokens, chans)
                value = value + jnp.dot(
                    left,
                    weights[m * chans : (m + 1) * chans, cols],
                    preferred_element_type=jnp.float32,
                )
            if d == nz:
                own[:, cols] = value
            else:
                sent[d - 1, :, cols] = value.astype(jnp.bfloat16)

        pl.loop(0, columns // tile)(strip)

    for step in range(nz + 2):
        if step < nz:
            d = step + 1
            k = plane(d)
            pltpu.make_async_copy(piece(k, c), piece(k, c), b_recv.at[k]).wait()
            each(1, chips, lambda i: spread(d, i).start())
            hand(d, 0).start()
        if 1 <= step <= nz:
            d = step

            def forward(i):
                k = plane(d)
                p = lax.rem(chip + i, chips)
                remote(
                    piece(k, c), piece(k, p * 2 + core), s_send.at[d - 1, i], s_recv.at[k, p], (z, mate)
                ).wait_recv()
                hand(d, i).start()

            each(1, chips, forward)
        if step >= 2:
            d = step - 1

            def collect(i):
                k = plane(d)
                p = lax.rem(chip + i, chips)
                remote(
                    piece(k, c), piece(k, p * 2 + 1 - core), m_send.at[d - 1, i], m_recv.at[k, p], (z, mate)
                ).wait_recv()

            each(0, chips, collect)
            if step == 2:
                w_copy.wait()
            multiply(d)
            if d < nz:
                back(d).start()

    for d in range(1, nz):
        back(d).wait_recv()

    def finish(i):
        span = pl.ds(pl.multiple_of(i * 32, 32), 32)
        value = own[span, :]
        for d in range(1, nz):
            value = value + taken[d - 1, span, :].astype(jnp.float32)
        out_ref[span, :] = value.astype(jnp.bfloat16)

    pl.loop(0, tokens // 32)(finish)

    each(1, nc, lambda i: scatter(i).wait_send())
    for d in range(1, nz):
        along(d).wait_send()
        back(d).wait_send()
    for d in range(1, nz + 1):
        each(1, chips, lambda i: spread(d, i).wait_send())
        each(0, chips, lambda i: hand(d, i).wait_send())


def per_device(nz, nc, features, short_weight, rates, residues, skip, out_weight):
    width = short_weight.shape[1]
    _, tokens, chans = features.shape
    modes = rates.shape[1]
    depth, columns = out_weight.shape
    subs = chans // LANES
    rows = tokens // nc
    fold = nc // nz
    chips = nc // 2
    f32, bf16 = jnp.float32, jnp.bfloat16
    vmem = pl.BlockSpec(memory_space=pltpu.VMEM)
    dma = pltpu.SemaphoreType.DMA

    gated = pl.pallas_call(
        functools.partial(operator_kernel, nz, modes, width),
        out_shape=jax.ShapeDtypeStruct((nc, rows, chans), bf16),
        in_specs=[vmem] * 5,
        out_specs=vmem,
        scratch_shapes=[
            pltpu.VMEM((3, RIM, chans), bf16),
            pltpu.VMEM((3, (tokens + HEAD) * subs, LANES), f32),
            pltpu.VMEM((tokens * subs, LANES), f32),
            pltpu.VMEM((tokens * subs, LANES), f32),
            pltpu.VMEM((tokens * subs, LANES), f32),
            pltpu.VMEM((modes * subs, LANES), f32),
            pltpu.VMEM((nz - 1, modes * subs, LANES), f32),
            dma, dma, dma((nz - 1,)), dma((nz - 1,)),
        ],
        compiler_params=pltpu.CompilerParams(
            collective_id=0, has_side_effects=True, vmem_limit_bytes=40 * 2**20
        ),
        name="operator",
    )(
        features,
        short_weight.reshape(3 * width * subs, LANES),
        rates.T.reshape(modes * subs, LANES),
        residues.T.reshape(modes * subs, LANES),
        skip.reshape(subs, LANES),
    )

    return pl.pallas_call(
        functools.partial(project_kernel, nz, nc),
        out_shape=jax.ShapeDtypeStruct((tokens, columns), bf16),
        in_specs=[vmem, pl.BlockSpec(memory_space=pl.ANY)],
        out_specs=vmem,
        scratch_shapes=[
            pltpu.VMEM((depth, columns), bf16),
            pltpu.VMEM((nc, rows, chans), bf16),
            pltpu.VMEM((nz, fold, nc, rows, chans), bf16),
            pltpu.VMEM((nz - 1, tokens, columns), bf16),
            pltpu.VMEM((nz - 1, tokens, columns), bf16),
            pltpu.VMEM((tokens, columns), f32),
            dma,
            dma((nc,)), dma((nc,)),
            dma((nz,)), dma((nz,)),
            dma((nz, chips)), dma((nz, chips)),
            dma((nz, chips)), dma((nz, chips)),
            dma((nz - 1,)), dma((nz - 1,)),
        ],
        compiler_params=pltpu.CompilerParams(
            collective_id=1, has_side_effects=True, vmem_limit_bytes=40 * 2**20
        ),
        name="project",
    )(gated, out_weight)


def solution(mesh):
    return jax.shard_map(
        functools.partial(per_device, mesh.shape["ctx"], mesh.shape["ch"]),
        mesh=mesh,
        in_specs=(
            P(None, "ctx", "ch"),
            P(None, None, "ch"),
            P("ch", None),
            P("ch", None),
            P("ch"),
            P("ctx", "ch"),
        ),
        out_specs=P("ctx", "ch"),
        check_vma=False,
    )
```

time: 509 us -> 110 us (0.22)
  waiting for transfers between devices: 323 us -> 0 us
  Pallas kernels: 0 us -> 101 us
  matrix products: 64.6 us -> 0 us
  local copies, waits for them, and re-layouts: 59.7 us -> 7.7 us
  blocking collectives: 26.9 us -> 0 us
  between operations: 13.6 us -> 0.04 us
  other arithmetic: 11.5 us -> 0 us
    all_gather x2 -> x0, waiting for transfers between devices: 323 us -> none  [the longest x1 285 us: per_device(): lax.all_gather(out_weight, 'ctx', axis=0, tiled=True)]
    pallas_call x0 -> x2, Pallas kernels: none -> 101 us  [the longest x1 87.2 us: per_device(): pl.pallas_call(functools.partial(project_kernel, nz, nc), out_shape=jax.S...]
    dot_general x4 -> x0, matrix products: 64.6 us -> none  [the longest x1 30 us: per_device(): inner_part = jnp.einsum('cab,kbc->kac', toeplitz, blocks, precision=highest)]
    gather x2 -> x0, local copies, waits for them, and re-layouts: 49.1 us -> none  [per_device(): short_filter[:, jnp.maximum(lag_table, 0)]]
    all_gather x2 -> x0, blocking collectives: 26.9 us -> none  [prefix_2(): everything = jax.tree.map(lambda part: lax.all_gather(part, axis), value)]
  transfers between devices with their start and end apart: 3 -> 0, of which waited for: 2 -> 0; matrix products, arithmetic and copies ran while one was open for 11% -> 0% of each run, Pallas kernels for 0% -> 0%
where the time goes in v1:
time: 110 us; the launch traced here: 108 us
  Pallas kernels  101 us (92%)
  local copies, waits for them, and re-layouts  7.7 us (7%)
    pallas_call x1, Pallas kernels, per_device(): pl.pallas_call(functools.partial(project_kernel, nz, nc), out_shape=jax.S...  87.2 us
    pallas_call x1, Pallas kernels, per_device(): pl.pallas_call(functools.partial(operator_kernel, nz, modes, width), out_...  13.3 us
    unnamed x7, local copies, waits for them, and re-layouts  5.07 us

profile of v1, /device:TPU:8, one launch (start us, length us, event | category | flops | bytes accessed | tf_op | source)
XLA Modules:
  0.0 108.3 jit_solution(12035207832237826005)
XLA Ops:
  0.0 0.9 reshape.13.rates_ref
  0.9 0.9 reshape.14.gains_ref
  1.7 0.9 reshape.12.taps_ref
  2.6 0.0 copy-start.1
  2.6 1.4 %copy-done.1 = bf16[3,256,1024]{2,1,0:T(8,128)(2,1)S(1)} copy-done((bf16[3,256,1024]{2,1,0:T(8,128)(2,1)S(1)}, bf16[3,256,1024]{2,1,0:T(8,128)(2,1)}, u32[]{:S(2)}) %copy-start.1) | copy-done | bytes 1572888
  4.0 0.0 copy-start.2
  4.1 0.7 copy-done.2
  4.7 13.3 %operator.1.g_ref = bf16[8,32,1024]{2,1,0:T(8,128)(2,1)S(1)} custom-call(bf16[3,256,1024]{2,1,0:T(8,128)(2,1)S(1)} %copy-done.1, f32[168,128]{1,0:T(8,128)S(1)} %reshape.12.taps_ref, f32[128,128]{1,0:T(8,128)S(1)} %reshape.13.rates_ref, f32[128,128]{1,0:T(8,128)S(1)} %reshape.14.gains_ref, f32[8,128]{1,0:T(8,128)S(1)} %bitcast.3), custom_call_target="tpu_custom_call" | custom-call | tf_op jit(solution)/shard_map/operator/pallas_call | solution.py:384
  18.0 0.0 copy-start
  18.1 2.2 %copy-done = bf16[2048,1024]{1,0:T(8,128)(2,1)S(1)} copy-done((bf16[2048,1024]{1,0:T(8,128)(2,1)S(1)}, bf16[2048,1024]{1,0:T(8,128)(2,1)}, u32[]{:S(2)}) %copy-start) | copy-done | bytes 4194328
  20.2 87.2 %project.1 = bf16[256,1024]{1,0:T(8,128)(2,1)S(1)} custom-call(bf16[8,32,1024]{2,1,0:T(8,128)(2,1)S(1)} %operator.1.g_ref, bf16[2048,1024]{1,0:T(8,128)(2,1)S(1)} %copy-done), custom_call_target="tpu_custom_call" | custom-call | tf_op jit(solution)/shard_map/project/pallas_call | solution.py:411
  107.5 0.8 copy.8
Async XLA Ops:
  2.6 1.4 %copy-start.1 = (bf16[3,256,1024]{2,1,0:T(8,128)(2,1)S(1)}, bf16[3,256,1024]{2,1,0:T(8,128)(2,1)}, u32[]{:S(2)}) copy-start(bf16[3,256,1024]{2,1,0:T(8,128)(2,1)} %feat_ref.1) | copy-start | bytes 4718596
  4.0 0.7 copy-start.2
  18.0 2.2 %copy-start = (bf16[2048,1024]{1,0:T(8,128)(2,1)S(1)}, bf16[2048,1024]{1,0:T(8,128)(2,1)}, u32[]{:S(2)}) copy-start(bf16[2048,1024]{1,0:T(8,128)(2,1)} %w_ref.1) | copy-start | bytes 12582916

commit v2 on v1

--- a/solution.py
+++ b/solution.py
@@ -11,6 +11,7 @@
 HEAD = 8
 RIM = 16
 UNROLL = 8
+CHUNKS = 2
 
 
 def each(low, high, body):
@@ -51,15 +52,22 @@
 
 def operator_kernel(
     nz, modes, width,
-    feat_ref, taps_ref, rates_ref, gains_ref, skip_ref,
+    feat_hbm, taps_in, rates_in, gains_in, skip_ref,
     out_ref,
+    feat_ref, taps_ref, rates_ref, gains_ref,
     rim, wide, product, query, gated, total, states,
-    rim_send, rim_recv, state_send, state_recv,
+    feat_sem, rim_send, rim_recv, state_send, state_recv,
 ):
     z, c = lax.axis_index("ctx"), lax.axis_index("ch")
-    tokens, chans = feat_ref.shape[1], feat_ref.shape[2]
+    tokens, chans = feat_hbm.shape[1], feat_hbm.shape[2]
     subs = chans // LANES
     parts, rows = out_ref.shape[0], out_ref.shape[1]
+
+    def load(s):
+        return pltpu.make_async_copy(feat_hbm.at[s], feat_ref.at[s], feat_sem.at[s])
+
+    for s in (1, 2, 0):
+        load(s).start()
 
     barrier = pltpu.get_barrier_semaphore()
 
@@ -69,10 +77,18 @@
         )
 
     each(1, nz, greet)
+
+    for g in range(subs):
+        lanes = slice(g * LANES, (g + 1) * LANES)
+        rates_ref[pl.ds(g, modes, stride=subs), :] = rates_in[:, lanes]
+        gains_ref[pl.ds(g, modes, stride=subs), :] = gains_in[:, lanes]
+        for s in range(3):
+            taps_ref[pl.ds(s * width * subs + g, width, stride=subs), :] = taps_in[s, :, lanes]
+
     pl.semaphore_wait(barrier, nz - 1)
 
     rim_copy = remote(
-        feat_ref.at[:, pl.ds(tokens - RIM, RIM), :], rim, rim_send, rim_recv,
+        feat_hbm.at[:, pl.ds(tokens - RIM, RIM), :], rim, rim_send, rim_recv,
         (lax.rem(z + 1, nz), c),
     )
 
@@ -80,11 +96,15 @@
     def _():
         rim_copy.start()
 
-    for s in range(3):
+    def unpack(s):
+        load(s).wait()
         for g in range(subs):
             wide[s, pl.ds(HEAD * subs + g, tokens, stride=subs), :] = feat_ref[
                 s, :, g * LANES : (g + 1) * LANES
             ].astype(jnp.float32)
+
+    unpack(1)
+    unpack(2)
 
     @pl.when(z > 0)
     def _():
@@ -140,6 +160,7 @@
 
     each(1, nz, pass_on)
 
+    unpack(0)
     taps_0 = taps_of(0)
 
     def second(i, carry):
@@ -251,44 +272,68 @@
     own_part.start()
     w_copy.start()
 
-    def plane(d):
-        return lax.rem(z + d, nz)
-
-    def along(d):
-        q = plane(d)
+    edges = jnp.minimum(z, nz - 1 - z)
+
+    def plane(s):
+        paired = nz - 1 - s // 2 if s % 2 == 0 else s // 2
+        single = jnp.where(2 * z < nz - 1, nz - 1 - s + edges, s - edges)
+        return jnp.where(s < 2 * edges, paired, single)
+
+    def along(s):
+        q = plane(s)
         src = stage.at[pl.ds(q * fold, fold)]
         dst = blocks.at[z, :, c]
-        if d == nz:
+        if s == nz - 1:
             return pltpu.make_async_copy(src, dst, b_recv.at[z])
-        return remote(src, dst, b_send.at[d], b_recv.at[z], (q, c))
-
-    for d in range(1, nz + 1):
+        return remote(src, dst, b_send.at[s], b_recv.at[z], (q, c))
+
+    for s in range(nz):
         for m in range(fold):
-            k = plane(d) * fold + m
+            k = plane(s) * fold + m
             pltpu.make_async_copy(g_ref.at[0], stage.at[k], a_recv.at[k]).wait()
-        along(d).start()
+        along(s).start()
 
     def piece(k, j):
         return blocks.at[k, :, j]
 
-    def spread(d, i):
-        k = plane(d)
+    def spread(s, i):
+        k = plane(s)
         to = lax.rem(chip + i, chips) * 2 + core
-        return remote(piece(k, c), piece(k, c), s_send.at[d - 1, i], s_recv.at[k, chip], (z, to))
-
-    def hand(d, i):
-        k = plane(d)
+        return remote(piece(k, c), piece(k, c), s_send.at[s, i], s_recv.at[k, chip], (z, to))
+
+    def hand(s, i):
+        k = plane(s)
         p = lax.rem(chip + i, chips)
         j = p * 2 + core
-        return remote(piece(k, j), piece(k, j), m_send.at[d - 1, i], m_recv.at[k, p], (z, mate))
-
-    def back(d):
+        return remote(piece(k, j), piece(k, j), m_send.at[s, i], m_recv.at[k, p], (z, mate))
+
+    def span(h):
+        return pl.ds(h * (tokens // CHUNKS), tokens // CHUNKS)
+
+    def back(s, h):
+        k = plane(s)
+        up = k > z
+        to = jnp.where(up, z + 1, z - 1)
+        slot = jnp.where(k == z - 1, nz, k)
         return remote(
-            sent.at[d - 1], taken.at[d - 1], p_send.at[d - 1], p_recv.at[d - 1], (plane(d), c)
+            sent.at[s, span(h)], taken.at[slot, span(h)], p_send.at[s, h], p_recv.at[slot, h], (to, c)
         )
 
-    def multiply(d):
-        k = plane(d)
+    def arrived(slot, h):
+        there = taken.at[slot, span(h)]
+        pltpu.make_async_copy(there, there, p_recv.at[slot, h]).wait()
+
+    def over(h, body):
+        each_rows = 32
+        base = h * (tokens // CHUNKS)
+
+        def go(i):
+            body(pl.ds(pl.multiple_of(base + i * each_rows, each_rows), each_rows))
+
+        pl.loop(0, tokens // CHUNKS // each_rows)(go)
+
+    def multiply(s):
+        k = plane(s)
 
         def strip(i):
             cols = pl.ds(pl.multiple_of(i * tile, tile), tile)
@@ -304,68 +349,92 @@
                     weights[m * chans : (m + 1) * chans, cols],
                     preferred_element_type=jnp.float32,
                 )
-            if d == nz:
-                own[:, cols] = value
-            else:
-                sent[d - 1, :, cols] = value.astype(jnp.bfloat16)
+            own[s, :, cols] = value
 
         pl.loop(0, columns // tile)(strip)
+
+    def begin(s):
+        def body(rows_at):
+            sent[s, rows_at, :] = own[s, rows_at, :].astype(jnp.bfloat16)
+
+        for h in range(CHUNKS):
+            over(h, body)
+            back(s, h).start()
+
+    def relay(s):
+        k = plane(s)
+
+        def body(rows_at):
+            value = own[s, rows_at, :] + taken[k, rows_at, :].astype(jnp.float32)
+            sent[s, rows_at, :] = value.astype(jnp.bfloat16)
+
+        for h in range(CHUNKS):
+            arrived(k, h)
+            over(h, body)
+            back(s, h).start()
 
     for step in range(nz + 2):
         if step < nz:
-            d = step + 1
-            k = plane(d)
+            s = step
+            k = plane(s)
             pltpu.make_async_copy(piece(k, c), piece(k, c), b_recv.at[k]).wait()
-            each(1, chips, lambda i: spread(d, i).start())
-            hand(d, 0).start()
+            each(1, chips, lambda i: spread(s, i).start())
+            hand(s, 0).start()
         if 1 <= step <= nz:
-            d = step
+            s = step - 1
 
             def forward(i):
-                k = plane(d)
+                k = plane(s)
                 p = lax.rem(chip + i, chips)
                 remote(
-                    piece(k, c), piece(k, p * 2 + core), s_send.at[d - 1, i], s_recv.at[k, p], (z, mate)
+                    piece(k, c), piece(k, p * 2 + core), s_send.at[s, i], s_recv.at[k, p], (z, mate)
                 ).wait_recv()
-                hand(d, i).start()
+                hand(s, i).start()
 
             each(1, chips, forward)
         if step >= 2:
-            d = step - 1
+            s = step - 2
 
             def collect(i):
-                k = plane(d)
+                k = plane(s)
                 p = lax.rem(chip + i, chips)
                 remote(
-                    piece(k, c), piece(k, p * 2 + 1 - core), m_send.at[d - 1, i], m_recv.at[k, p], (z, mate)
+                    piece(k, c), piece(k, p * 2 + 1 - core), m_send.at[s, i], m_recv.at[k, p], (z, mate)
                 ).wait_recv()
 
             each(0, chips, collect)
             if step == 2:
                 w_copy.wait()
-            multiply(d)
-            if d < nz:
-                back(d).start()
-
-    for d in range(1, nz):
-        back(d).wait_recv()
-
-    def finish(i):
-        span = pl.ds(pl.multiple_of(i * 32, 32), 32)
-        value = own[span, :]
-        for d in range(1, nz):
-            value = value + taken[d - 1, span, :].astype(jnp.float32)
-        out_ref[span, :] = value.astype(jnp.bfloat16)
-
-    pl.loop(0, tokens // 32)(finish)
+            multiply(s)
+            if s < nz - 1:
+                pl.when(edges == 0)(functools.partial(begin, s))
+        if 3 <= step:
+            pl.when(edges > 0)(functools.partial(relay, step - 3))
+
+    def join(slot, h):
+        arrived(slot, h)
+
+        def body(rows_at):
+            own[nz - 1, rows_at, :] += taken[slot, rows_at, :].astype(jnp.float32)
+
+        over(h, body)
+
+    def finish(rows_at):
+        out_ref[rows_at, :] = own[nz - 1, rows_at, :].astype(jnp.bfloat16)
+
+    for h in range(CHUNKS):
+        pl.when(z > 0)(functools.partial(join, z, h))
+        pl.when(z < nz - 1)(functools.partial(join, nz, h))
+        over(h, finish)
 
     each(1, nc, lambda i: scatter(i).wait_send())
-    for d in range(1, nz):
-        along(d).wait_send()
-        back(d).wait_send()
-    for d in range(1, nz + 1):
-        each(1, chips, lambda i: spread(d, i).wait_send())
-        each(0, chips, lambda i: hand(d, i).wait_send())
+    for s in range(nz - 1):
+        along(s).wait_send()
+        for h in range(CHUNKS):
+            back(s, h).wait_send()
+    for s in range(nz):
+        each(1, chips, lambda i: spread(s, i).wait_send())
+        each(0, chips, lambda i: hand(s, i).wait_send())
 
 
 def per_device(nz, nc, features, short_weight, rates, residues, skip, out_weight):
@@ -379,14 +448,19 @@
     chips = nc // 2
     f32, bf16 = jnp.float32, jnp.bfloat16
     vmem = pl.BlockSpec(memory_space=pltpu.VMEM)
+    hbm = pl.BlockSpec(memory_space=pltpu.HBM)
     dma = pltpu.SemaphoreType.DMA
 
     gated = pl.pallas_call(
         functools.partial(operator_kernel, nz, modes, width),
         out_shape=jax.ShapeDtypeStruct((nc, rows, chans), bf16),
-        in_specs=[vmem] * 5,
+        in_specs=[hbm] + [vmem] * 4,
         out_specs=vmem,
         scratch_shapes=[
+            pltpu.VMEM((3, tokens, chans), bf16),
+            pltpu.VMEM((3 * width * subs, LANES), f32),
+            pltpu.VMEM((modes * subs, LANES), f32),
+            pltpu.VMEM((modes * subs, LANES), f32),
             pltpu.VMEM((3, RIM, chans), bf16),
             pltpu.VMEM((3, (tokens + HEAD) * subs, LANES), f32),
             pltpu.VMEM((tokens * subs, LANES), f32),
@@ -394,7 +468,7 @@
             pltpu.VMEM((tokens * subs, LANES), f32),
             pltpu.VMEM((modes * subs, LANES), f32),
             pltpu.VMEM((nz - 1, modes * subs, LANES), f32),
-            dma, dma, dma((nz - 1,)), dma((nz - 1,)),
+            dma((3,)), dma, dma, dma((nz - 1,)), dma((nz - 1,)),
         ],
         compiler_params=pltpu.CompilerParams(
             collective_id=0, has_side_effects=True, vmem_limit_bytes=40 * 2**20
@@ -402,30 +476,30 @@
         name="operator",
     )(
         features,
-        short_weight.reshape(3 * width * subs, LANES),
-        rates.T.reshape(modes * subs, LANES),
-        residues.T.reshape(modes * subs, LANES),
+        short_weight,
+        rates.T,
+        residues.T,
         skip.reshape(subs, LANES),
     )
 
     return pl.pallas_call(
         functools.partial(project_kernel, nz, nc),
         out_shape=jax.ShapeDtypeStruct((tokens, columns), bf16),
-        in_specs=[vmem, pl.BlockSpec(memory_space=pl.ANY)],
+        in_specs=[vmem, hbm],
         out_specs=vmem,
         scratch_shapes=[
             pltpu.VMEM((depth, columns), bf16),
             pltpu.VMEM((nc, rows, chans), bf16),
             pltpu.VMEM((nz, fold, nc, rows, chans), bf16),
             pltpu.VMEM((nz - 1, tokens, columns), bf16),
-            pltpu.VMEM((nz - 1, tokens, columns), bf16),
-            pltpu.VMEM((tokens, columns), f32),
+            pltpu.VMEM((nz + 1, tokens, columns), bf16),
+            pltpu.VMEM((nz, tokens, columns), f32),
             dma,
             dma((nc,)), dma((nc,)),
             dma((nz,)), dma((nz,)),
             dma((nz, chips)), dma((nz, chips)),
             dma((nz, chips)), dma((nz, chips)),
-            dma((nz - 1,)), dma((nz - 1,)),
+            dma((nz - 1, CHUNKS)), dma((nz + 1, CHUNKS)),
         ],
         compiler_params=pltpu.CompilerParams(
             collective_id=1, has_side_effects=True, vmem_limit_bytes=40 * 2**20

time: 110 us -> 107 us (0.973)
  Pallas kernels: 101 us -> 97.6 us
    pallas_call x1, Pallas kernels: 87.2 us -> 84.1 us  [per_device(): pl.pallas_call(functools.partial(project_kernel, nz, nc), out_shape=jax.S...]
    reshape x3 -> x0, local copies, waits for them, and re-layouts: 2.63 us -> none  [the longest x1 0.91 us: per_device(): short_weight.reshape(3 * width * subs, LANES)]
    unnamed x7 -> x13, local copies, waits for them, and re-layouts: 5.07 us -> 7.64 us
where the time goes in v2:
time: 107 us; the launch traced here: 105 us
  Pallas kernels  97.6 us (91%)
  local copies, waits for them, and re-layouts  7.64 us (7%)
    pallas_call x1, Pallas kernels, per_device(): pl.pallas_call(functools.partial(project_kernel, nz, nc), out_shape=jax.S...  84.1 us
    pallas_call x1, Pallas kernels, per_device(): pl.pallas_call(functools.partial(operator_kernel, nz, modes, width), out_...  13.6 us
    unnamed x13, local copies, waits for them, and re-layouts  7.64 us

profile of v2, /device:TPU:8, one launch (start us, length us, event | category | flops | bytes accessed | tf_op | source)
XLA Modules:
  0.0 105.3 jit_solution(4374276270112404453)
XLA Ops:
  0.0 0.0 copy-start.1
  0.0 1.4 %copy-done.1 = bf16[3,256,1024]{2,1,0:T(8,128)(2,1)S(1)} copy-done((bf16[3,256,1024]{2,1,0:T(8,128)(2,1)S(1)}, bf16[3,256,1024]{2,1,0:T(8,128)(2,1)}, u32[]{:S(2)}) %copy-start.1) | copy-done | bytes 1572888
  1.4 0.0 copy-start.2
  1.4 0.9 copy-done.2
  2.3 0.0 copy-start.3
  2.3 0.8 copy-done.3
  3.1 0.0 copy-start.4
  3.1 0.8 copy-done.4
  4.0 0.0 copy-start.5
  4.0 0.7 copy-done.5
  4.7 13.6 %operator.1.g_ref = bf16[8,32,1024]{2,1,0:T(8,128)(2,1)S(1)} custom-call(bf16[3,256,1024]{2,1,0:T(8,128)(2,1)S(1)} %copy-done.1, f32[3,7,1024]{2,1,0:T(8,128)S(1)} %copy-done.2, f32[16,1024]{1,0:T(8,128)S(1)} %bitcast.3, f32[16,1024]{1,0:T(8,128)S(1)} %bitcast.4, f32[8,128]{1,0:T(8,128)S(1)} %bitcast.5), custom_call_target="tpu_custom_call" | custom-call | tf_op jit(solution)/shard_map/operator/pallas_call | solution.py:454
  18.2 0.0 copy-start
  18.2 2.2 %copy-done = bf16[2048,1024]{1,0:T(8,128)(2,1)S(1)} copy-done((bf16[2048,1024]{1,0:T(8,128)(2,1)S(1)}, bf16[2048,1024]{1,0:T(8,128)(2,1)}, u32[]{:S(2)}) %copy-start) | copy-done | bytes 4194328
  20.4 84.1 %project.1 = bf16[256,1024]{1,0:T(8,128)(2,1)S(1)} custom-call(bf16[8,32,1024]{2,1,0:T(8,128)(2,1)S(1)} %operator.1.g_ref, bf16[2048,1024]{1,0:T(8,128)(2,1)S(1)} %copy-done), custom_call_target="tpu_custom_call" | custom-call | tf_op jit(solution)/shard_map/project/pallas_call | solution.py:485
  104.5 0.8 copy.8
Async XLA Ops:
  0.0 1.4 %copy-start.1 = (bf16[3,256,1024]{2,1,0:T(8,128)(2,1)S(1)}, bf16[3,256,1024]{2,1,0:T(8,128)(2,1)}, u32[]{:S(2)}) copy-start(bf16[3,256,1024]{2,1,0:T(8,128)(2,1)} %feat_hbm.1) | copy-start | bytes 4718596
  1.4 0.9 copy-start.2
  2.3 0.8 copy-start.3
  3.1 0.8 copy-start.4
  4.0 0.7 copy-start.5
  18.2 2.2 %copy-start = (bf16[2048,1024]{1,0:T(8,128)(2,1)S(1)}, bf16[2048,1024]{1,0:T(8,128)(2,1)}, u32[]{:S(2)}) copy-start(bf16[2048,1024]{1,0:T(8,128)(2,1)} %w_ref.1) | copy-start | bytes 12582916

commit v3 on v2

--- a/solution.py
+++ b/solution.py
@@ -51,32 +51,58 @@
 
 
 def operator_kernel(
-    nz, modes, width,
-    feat_hbm, taps_in, rates_in, gains_in, skip_ref,
+    nz, nc, modes, width,
+    feat_hbm, taps_hbm, rates_hbm, gains_hbm, skip_hbm, w_ref,
     out_ref,
-    feat_ref, taps_ref, rates_ref, gains_ref,
+    feat_ref, taps_in, rates_in, gains_in, skip_ref, taps_ref, rates_ref, gains_ref,
     rim, wide, product, query, gated, total, states,
-    feat_sem, rim_send, rim_recv, state_send, state_recv,
+    g_ref, weights, stage, blocks, sent, taken, own,
+    feat_sem, rim_send, rim_recv, state_send, state_recv, small_sem,
+    w_sem, a_send, a_recv, b_send, b_recv, s_send, s_recv, m_send, m_recv, p_send, p_recv,
 ):
     z, c = lax.axis_index("ctx"), lax.axis_index("ch")
     tokens, chans = feat_hbm.shape[1], feat_hbm.shape[2]
     subs = chans // LANES
-    parts, rows = out_ref.shape[0], out_ref.shape[1]
+    rows = g_ref.shape[1]
+    columns = out_ref.shape[1]
+    fold = nc // nz
+    chips = nc // 2
+    chip, core = c // 2, lax.rem(c, 2)
+    mate = c + 1 - 2 * core
+    tile = min(columns, 256)
 
     def load(s):
         return pltpu.make_async_copy(feat_hbm.at[s], feat_ref.at[s], feat_sem.at[s])
 
-    for s in (1, 2, 0):
-        load(s).start()
+    small = [
+        pltpu.make_async_copy(src, dst, small_sem.at[i])
+        for i, (src, dst) in enumerate(
+            ((taps_hbm, taps_in), (rates_hbm, rates_in), (gains_hbm, gains_in), (skip_hbm, skip_ref))
+        )
+    ]
+    w_copy = pltpu.make_async_copy(w_ref, weights, w_sem)
 
     barrier = pltpu.get_barrier_semaphore()
 
-    def greet(d):
+    def greet_line(d):
         pl.semaphore_signal(
             barrier, inc=1, device_id=(lax.rem(z + d, nz), c), device_id_type=MESH
         )
 
-    each(1, nz, greet)
+    def greet_plane(i):
+        pl.semaphore_signal(
+            barrier, inc=1, device_id=(z, lax.rem(c + i, nc)), device_id_type=MESH
+        )
+
+    each(1, nz, greet_line)
+    each(1, nc, greet_plane)
+    for copy in small:
+        copy.start()
+    for s in (1, 2, 0):
+        load(s).start()
+    w_copy.start()
+    for copy in small:
+        copy.wait()
 
     for g in range(subs):
         lanes = slice(g * LANES, (g + 1) * LANES)
@@ -85,7 +111,7 @@
         for s in range(3):
             taps_ref[pl.ds(s * width * subs + g, width, stride=subs), :] = taps_in[s, :, lanes]
 
-    pl.semaphore_wait(barrier, nz - 1)
+    pl.semaphore_wait(barrier, nc + nz - 2)
 
     rim_copy = remote(
         feat_hbm.at[:, pl.ds(tokens - RIM, RIM), :], rim, rim_send, rim_recv,
@@ -196,81 +222,37 @@
     gains = [gains_ref[at(n), :] for n in range(modes)]
     skip = skip_ref[...]
 
-    def third(i, carry):
-        carry = list(carry)
-        for u in range(UNROLL):
-            t = i * UNROLL + u
-            value = product[token(t), :]
-            carry = [k * m + value for k, m in zip(decay, carry)]
-            conv = added([g * m for g, m in zip(gains, carry)] + [skip * value])
-            gated[token(t), :] = query[token(t), :] * conv
-        return tuple(carry)
-
-    lax.fori_loop(0, tokens // UNROLL, third, tuple(incoming))
-
-    for j in range(parts):
+    def scatter(j):
+        return remote(g_ref.at[j], stage.at[c], a_send.at[j], a_recv.at[c], (z, j))
+
+    def portion(j, carry):
+        def third(i, carry):
+            carry = list(carry)
+            for u in range(UNROLL):
+                t = j * rows + i * UNROLL + u
+                value = product[token(t), :]
+                carry = [k * m + value for k, m in zip(decay, carry)]
+                conv = added([g * m for g, m in zip(gains, carry)] + [skip * value])
+                gated[token(i * UNROLL + u), :] = query[token(t), :] * conv
+            return tuple(carry)
+
+        carry = lax.fori_loop(0, rows // UNROLL, third, carry)
         for g in range(subs):
-            out_ref[j, :, g * LANES : (g + 1) * LANES] = gated[
-                pl.ds(j * rows * subs + g, rows, stride=subs), :
+            g_ref[j, :, g * LANES : (g + 1) * LANES] = gated[
+                pl.ds(g, rows, stride=subs), :
             ].astype(jnp.bfloat16)
 
-    @pl.when(z < nz - 1)
-    def _():
-        rim_copy.wait_send()
-
-    def leave(d):
-        @pl.when(z + d < nz)
+        @pl.when(j != c)
         def _():
-            remote(
-                total, states.at[d - 1], state_send.at[d - 1], state_recv.at[d - 1],
-                (lax.rem(z + d, nz), c),
-            ).wait_send()
-
-    each(1, nz, leave)
-
-
-def project_kernel(
-    nz, nc,
-    g_ref, w_ref,
-    out_ref,
-    weights, stage, blocks, sent, taken, own,
-    w_sem, a_send, a_recv, b_send, b_recv, s_send, s_recv, m_send, m_recv, p_send, p_recv,
-):
-    z, c = lax.axis_index("ctx"), lax.axis_index("ch")
-    fold = nc // nz
-    chips = nc // 2
-    chip, core = c // 2, lax.rem(c, 2)
-    mate = c + 1 - 2 * core
-    tokens, columns = out_ref.shape
-    rows, chans = g_ref.shape[1], g_ref.shape[2]
-    tile = min(columns, 256)
-
-    barrier = pltpu.get_barrier_semaphore()
-
-    def greet_plane(i):
-        pl.semaphore_signal(
-            barrier, inc=1, device_id=(z, lax.rem(c + i, nc)), device_id_type=MESH
-        )
-
-    def greet_line(d):
-        pl.semaphore_signal(
-            barrier, inc=1, device_id=(lax.rem(z + d, nz), c), device_id_type=MESH
-        )
-
-    each(1, nc, greet_plane)
-    each(1, nz, greet_line)
-    pl.semaphore_wait(barrier, nc + nz - 2)
-
-    w_copy = pltpu.make_async_copy(w_ref, weights, w_sem)
-
-    def scatter(i):
-        j = lax.rem(c + i, nc)
-        return remote(g_ref.at[j], stage.at[c], a_send.at[i], a_recv.at[c], (z, j))
-
-    each(1, nc, lambda i: scatter(i).start())
-    own_part = pltpu.make_async_copy(g_ref.at[c], stage.at[c], a_recv.at[c])
-    own_part.start()
-    w_copy.start()
+            scatter(j).start()
+
+        @pl.when(j == c)
+        def _():
+            pltpu.make_async_copy(g_ref.at[c], stage.at[c], a_recv.at[c]).start()
+
+        return carry
+
+    lax.fori_loop(0, nc, portion, tuple(incoming))
 
     edges = jnp.minimum(z, nz - 1 - z)
 
@@ -287,11 +269,12 @@
             return pltpu.make_async_copy(src, dst, b_recv.at[z])
         return remote(src, dst, b_send.at[s], b_recv.at[z], (q, c))
 
-    for s in range(nz):
-        for m in range(fold):
-            k = plane(s) * fold + m
-            pltpu.make_async_copy(g_ref.at[0], stage.at[k], a_recv.at[k]).wait()
-        along(s).start()
+    def send_along():
+        for s in range(nz):
+            for m in range(fold):
+                k = plane(s) * fold + m
+                pltpu.make_async_copy(g_ref.at[0], stage.at[k], a_recv.at[k]).wait()
+            along(s).start()
 
     def piece(k, j):
         return blocks.at[k, :, j]
@@ -373,43 +356,50 @@
             over(h, body)
             back(s, h).start()
 
-    for step in range(nz + 2):
-        if step < nz:
-            s = step
-            k = plane(s)
-            pltpu.make_async_copy(piece(k, c), piece(k, c), b_recv.at[k]).wait()
-            each(1, chips, lambda i: spread(s, i).start())
-            hand(s, 0).start()
-        if 1 <= step <= nz:
-            s = step - 1
-
-            def forward(i):
-                k = plane(s)
-                p = lax.rem(chip + i, chips)
-                remote(
-                    piece(k, c), piece(k, p * 2 + core), s_send.at[s, i], s_recv.at[k, p], (z, mate)
-                ).wait_recv()
-                hand(s, i).start()
-
-            each(1, chips, forward)
-        if step >= 2:
-            s = step - 2
-
-            def collect(i):
-                k = plane(s)
-                p = lax.rem(chip + i, chips)
-                remote(
-                    piece(k, c), piece(k, p * 2 + 1 - core), m_send.at[s, i], m_recv.at[k, p], (z, mate)
-                ).wait_recv()
-
-            each(0, chips, collect)
-            if step == 2:
-                w_copy.wait()
-            multiply(s)
-            if s < nz - 1:
-                pl.when(edges == 0)(functools.partial(begin, s))
-        if 3 <= step:
-            pl.when(edges > 0)(functools.partial(relay, step - 3))
+    def begin_block(s):
+        k = plane(s)
+        pltpu.make_async_copy(piece(k, c), piece(k, c), b_recv.at[k]).wait()
+        each(1, chips, lambda i: spread(s, i).start())
+        hand(s, 0).start()
+
+    def forward_block(s):
+        k = plane(s)
+
+        def forward(i):
+            p = lax.rem(chip + i, chips)
+            remote(
+                piece(k, c), piece(k, p * 2 + core), s_send.at[s, i], s_recv.at[k, p], (z, mate)
+            ).wait_recv()
+            hand(s, i).start()
+
+        each(1, chips, forward)
+
+    def collect_block(s):
+        k = plane(s)
+
+        def collect(i):
+            p = lax.rem(chip + i, chips)
+            remote(
+                piece(k, c), piece(k, p * 2 + 1 - core), m_send.at[s, i], m_recv.at[k, p], (z, mate)
+            ).wait_recv()
+
+        each(0, chips, collect)
+
+    pl.when(edges == 0)(send_along)
+    begin_block(0)
+    pl.when(edges > 0)(send_along)
+    for s in range(nz):
+        forward_block(s)
+        if s < nz - 1:
+            begin_block(s + 1)
+        collect_block(s)
+        if s == 0:
+            w_copy.wait()
+        multiply(s)
+        if s < nz - 1:
+            pl.when(edges == 0)(functools.partial(begin, s))
+        if s > 0:
+            pl.when(edges > 0)(functools.partial(relay, s - 1))
 
     def join(slot, h):
         arrived(slot, h)
@@ -427,7 +417,20 @@
         pl.when(z < nz - 1)(functools.partial(join, nz, h))
         over(h, finish)
 
-    each(1, nc, lambda i: scatter(i).wait_send())
+    @pl.when(z < nz - 1)
+    def _():
+        rim_copy.wait_send()
+
+    def leave(d):
+        @pl.when(z + d < nz)
+        def _():
+            remote(
+                total, states.at[d - 1], state_send.at[d - 1], state_recv.at[d - 1],
+                (lax.rem(z + d, nz), c),
+            ).wait_send()
+
+    each(1, nz, leave)
+    each(1, nc, lambda i: scatter(lax.rem(c + i, nc)).wait_send())
     for s in range(nz - 1):
         along(s).wait_send()
         for h in range(CHUNKS):
@@ -451,13 +454,17 @@
     hbm = pl.BlockSpec(memory_space=pltpu.HBM)
     dma = pltpu.SemaphoreType.DMA
 
-    gated = pl.pallas_call(
-        functools.partial(operator_kernel, nz, modes, width),
-        out_shape=jax.ShapeDtypeStruct((nc, rows, chans), bf16),
-        in_specs=[hbm] + [vmem] * 4,
+    return pl.pallas_call(
+        functools.partial(operator_kernel, nz, nc, modes, width),
+        out_shape=jax.ShapeDtypeStruct((tokens, columns), bf16),
+        in_specs=[hbm] * 6,
         out_specs=vmem,
         scratch_shapes=[
             pltpu.VMEM((3, tokens, chans), bf16),
+            pltpu.VMEM((3, width, chans), f32),
+            pltpu.VMEM((modes, chans), f32),
+            pltpu.VMEM((modes, chans), f32),
+            pltpu.VMEM((subs, LANES), f32),
             pltpu.VMEM((3 * width * subs, LANES), f32),
             pltpu.VMEM((modes * subs, LANES), f32),
             pltpu.VMEM((modes * subs, LANES), f32),
@@ -465,35 +472,17 @@
             pltpu.VMEM((3, (tokens + HEAD) * subs, LANES), f32),
             pltpu.VMEM((tokens * subs, LANES), f32),
             pltpu.VMEM((tokens * subs, LANES), f32),
-            pltpu.VMEM((tokens * subs, LANES), f32),
+            pltpu.VMEM((rows * subs, LANES), f32),
             pltpu.VMEM((modes * subs, LANES), f32),
             pltpu.VMEM((nz - 1, modes * subs, LANES), f32),
-            dma((3,)), dma, dma, dma((nz - 1,)), dma((nz - 1,)),
-        ],
-        compiler_params=pltpu.CompilerParams(
-            collective_id=0, has_side_effects=True, vmem_limit_bytes=40 * 2**20
-        ),
-        name="operator",
-    )(
-        features,
-        short_weight,
-        rates.T,
-        residues.T,
-        skip.reshape(subs, LANES),
-    )
-
-    return pl.pallas_call(
-        functools.partial(project_kernel, nz, nc),
-        out_shape=jax.ShapeDtypeStruct((tokens, columns), bf16),
-        in_specs=[vmem, hbm],
-        out_specs=vmem,
-        scratch_shapes=[
+            pltpu.VMEM((nc, rows, chans), bf16),
             pltpu.VMEM((depth, columns), bf16),
             pltpu.VMEM((nc, rows, chans), bf16),
             pltpu.VMEM((nz, fold, nc, rows, chans), bf16),
             pltpu.VMEM((nz - 1, tokens, columns), bf16),
             pltpu.VMEM((nz + 1, tokens, columns), bf16),
             pltpu.VMEM((nz, tokens, columns), f32),
+            dma((3,)), dma, dma, dma((nz - 1,)), dma((nz - 1,)), dma((4,)),
             dma,
             dma((nc,)), dma((nc,)),
             dma((nz,)), dma((nz,)),
@@ -502,10 +491,10 @@
             dma((nz - 1, CHUNKS)), dma((nz + 1, CHUNKS)),
         ],
         compiler_params=pltpu.CompilerParams(
-            collective_id=1, has_side_effects=True, vmem_limit_bytes=40 * 2**20
+            collective_id=0, has_side_effects=True, vmem_limit_bytes=62 * 2**20
         ),
-        name="project",
-    )(gated, out_weight)
+        name="operator",
+    )(features, short_weight, rates.T, residues.T, skip.reshape(subs, LANES), out_weight)
 
 
 def solution(mesh):

time: 107 us -> 98.7 us (0.922)
  the two profiles are of different devices: /device:TPU:8 before, /device:TPU:17 now
where the time goes in v3:
time: 98.7 us; the launch traced here: 98.5 us
  Pallas kernels  96.7 us (98%)
  local copies, waits for them, and re-layouts  1.87 us (2%)
    pallas_call x1, Pallas kernels, per_device(): pl.pallas_call(functools.partial(operator_kernel, nz, nc, modes, width),...  96.7 us

profile of v3, /device:TPU:17, one launch (start us, length us, event | category | flops | bytes accessed | tf_op | source)
XLA Modules:
  0.0 98.5 jit_solution(17939366431687484836)
XLA Ops:
  0.0 96.7 %operator.1 = bf16[256,1024]{1,0:T(8,128)(2,1)} custom-call(bf16[3,256,1024]{2,1,0:T(8,128)(2,1)} %feat_hbm.1, f32[3,7,1024]{2,1,0:T(8,128)} %taps_hbm.1, f32[16,1024]{1,0:T(8,128)} %bitcast.3, f32[16,1024]{1,0:T(8,128)} %bitcast.4, f32[8,128]{1,0:T(8,128)} %bitcast.5, bf16[2048,1024]{1,0:T(8,128)(2,1)} %w_ref.1), custom_call_target="tpu_custom_call" | custom-call | tf_op jit(solution)/shard_map/operator/pallas_call | solution.py:457
  96.7 1.9 %copy.8 = bf16[256,1024]{1,0:T(8,128)(2,1)} copy(bf16[256,1024]{1,0:T(8,128)(2,1)} %operator.1) | data formatting | bytes 1048576

commit v4 on v3

--- a/solution.py
+++ b/solution.py
@@ -257,7 +257,8 @@
     edges = jnp.minimum(z, nz - 1 - z)
 
     def plane(s):
-        paired = nz - 1 - s // 2 if s % 2 == 0 else s // 2
+        far = (nz - 1 - s // 2, s // 2)
+        paired = jnp.where(2 * z < nz - 1, far[s % 2], far[1 - s % 2])
         single = jnp.where(2 * z < nz - 1, nz - 1 - s + edges, s - edges)
         return jnp.where(s < 2 * edges, paired, single)
 

time: 98.7 us -> 82 us (0.83)
  the two profiles are of different devices: /device:TPU:17 before, /device:TPU:8 now
where the time goes in v4:
time: 82 us; the launch traced here: 81.9 us
  Pallas kernels  80 us (98%)
  local copies, waits for them, and re-layouts  1.87 us (2%)
    pallas_call x1, Pallas kernels, per_device(): pl.pallas_call(functools.partial(operator_kernel, nz, nc, modes, width),...  80 us
    unnamed x1, local copies, waits for them, and re-layouts  1.87 us

profile of v4, /device:TPU:8, one launch (start us, length us, event | category | flops | bytes accessed | tf_op | source)
XLA Modules:
  0.0 81.9 jit_solution(14894976493004190388)
XLA Ops:
  0.0 80.0 %operator.1 = bf16[256,1024]{1,0:T(8,128)(2,1)} custom-call(bf16[3,256,1024]{2,1,0:T(8,128)(2,1)} %feat_hbm.1, f32[3,7,1024]{2,1,0:T(8,128)} %taps_hbm.1, f32[16,1024]{1,0:T(8,128)} %bitcast.3, f32[16,1024]{1,0:T(8,128)} %bitcast.4, f32[8,128]{1,0:T(8,128)} %bitcast.5, bf16[2048,1024]{1,0:T(8,128)(2,1)} %w_ref.1), custom_call_target="tpu_custom_call" | custom-call | tf_op jit(solution)/shard_map/operator/pallas_call | solution.py:458
  80.0 1.9 %copy.8 = bf16[256,1024]{1,0:T(8,128)(2,1)} copy(bf16[256,1024]{1,0:T(8,128)(2,1)} %operator.1) | data formatting | bytes 1048576

commit v5 on v4

--- a/solution.py
+++ b/solution.py
@@ -11,7 +11,7 @@
 HEAD = 8
 RIM = 16
 UNROLL = 8
-CHUNKS = 2
+CHUNKS = 4
 
 
 def each(low, high, body):

time: 82 us -> 82 us (level)
  no operation moved by 1% of the time
where the time goes in v5:
time: 82 us; the launch traced here: 81.9 us
  Pallas kernels  80 us (98%)
  local copies, waits for them, and re-layouts  1.87 us (2%)
    pallas_call x1, Pallas kernels, per_device(): pl.pallas_call(functools.partial(operator_kernel, nz, nc, modes, width),...  80 us
    unnamed x1, local copies, waits for them, and re-layouts  1.87 us

profile of v5, /device:TPU:8, one launch (start us, length us, event | category | flops | bytes accessed | tf_op | source)
XLA Modules:
  0.0 81.9 jit_solution(8602806243840991326)
XLA Ops:
  0.0 80.0 %operator.1 = bf16[256,1024]{1,0:T(8,128)(2,1)} custom-call(bf16[3,256,1024]{2,1,0:T(8,128)(2,1)} %feat_hbm.1, f32[3,7,1024]{2,1,0:T(8,128)} %taps_hbm.1, f32[16,1024]{1,0:T(8,128)} %bitcast.3, f32[16,1024]{1,0:T(8,128)} %bitcast.4, f32[8,128]{1,0:T(8,128)} %bitcast.5, bf16[2048,1024]{1,0:T(8,128)(2,1)} %w_ref.1), custom_call_target="tpu_custom_call" | custom-call | tf_op jit(solution)/shard_map/operator/pallas_call | solution.py:458
  80.0 1.9 %copy.8 = bf16[256,1024]{1,0:T(8,128)(2,1)} copy(bf16[256,1024]{1,0:T(8,128)(2,1)} %operator.1) | data formatting | bytes 1048576
